TPU v7x, 128 devices: a whole 4x4x4 slice. The times are simulated.
128 devices in a mesh: ctx: 8 (over z, core), exp: 16 (over x, y).
Axes of the slice: x: 4, y: 4, z: 4, core: 2. Of those that a mesh axis runs over, the one named last changes fastest.
Arguments:
- queries: bfloat16 [16, 1024, 4096], P('exp', 'ctx'), may hold values from -100 to 100
- keys: bfloat16 [16, 1024, 256], P('exp', 'ctx'), may hold values from -12 to 12
- values: bfloat16 [16, 1024, 256], P('exp', 'ctx'), may hold values from -6 to 6
- residual: bfloat16 [16, 1024, 4096], P('exp', 'ctx'), may hold values from -6 to 6
- out_weight: bfloat16 [4096, 4096], P('ctx'), may hold values from -0.09375 to 0.09375
- norm_gain: float32 [4096], replicated, may hold values from 0.5 to 1.5
- expert_ids: int32 [16, 1024, 8], P('exp', 'ctx'), may hold values from 0 to 127, as said below
- gate_weights: float32 [16, 1024, 8], P('exp', 'ctx'), may hold values from 0.2 to 1
- slots: int32 [16, 1024, 8], P('exp', 'ctx'), may hold values from -1 to 3, as said below
- w_gate: bfloat16 [16, 4096, 1536], P('exp', None, 'ctx'), may hold values from -0.09375 to 0.09375
- w_up: bfloat16 [16, 4096, 1536], P('exp', None, 'ctx'), may hold values from -0.09375 to 0.09375
- w_down: bfloat16 [16, 1536, 4096], P('exp', 'ctx'), may hold values from -0.15625 to 0.15625
Outputs:
- attended: bfloat16 [16, 1024, 4096], P('exp', 'ctx')
- layer_out: bfloat16 [16, 1024, 4096], P('exp', 'ctx')
Inputs may be any that keep to these rules, and one draw needn't show every extreme that they name: `expert_ids`: each token names 8 different experts. Within one block of 128 positions, the choices of each expert below 16, taken in order of position and then of k, get slots 0, 1, 2 and so on; choices past 4 - 1 and choices of experts 16 or above get -1. Some expert fills all 4 slots in every block.
All inputs are finite; a program needn't handle non-finite values.
Results may differ from a plain program's by a relative error of at most 0.015.
Values may be sent and summed in bfloat16 or wider, within the bound.
A program may use at most 64 MiB of HBM per device.

v0:
```python
import functools

import jax
import jax.numpy as jnp
from jax import lax
from jax.experimental import pallas as pl
from jax.experimental.pallas import tpu as pltpu
from jax.sharding import PartitionSpec as P

D = 4096
HD = 128
QH = 32
TOK = 128
NZ = 4
HEADS = QH // NZ
HW = HEADS * HD
SEQ = 1024
FF_DEV = 192
FF_CHIP = 2 * FF_DEV
K_DEV = 512
CAP = 4
ROWS = 64
SCALE_COLS = 128
NCH = 4
CW = D // NCH
DX = D + SCALE_COLS
HALF = D // 2
QW = HALF // 4
BLOCKS = 16
EW = CW // 4
STACK = 4 * ROWS
F32 = jnp.float32
BF16 = jnp.bfloat16
MESH = pl.DeviceIdType.MESH

NT = (((1,), (1,)), ((), ()))


def cols(j):
    return pl.ds(j * CW, CW)


def xcols(j):
    return pl.ds(j * CW, CW + (SCALE_COLS if j == NCH - 1 else 0))


def qcols(p):
    return pl.ds(p * QW, QW + (SCALE_COLS if p == 1 else 0))


_count = 0


def _take(n):
    global _count
    first = _count
    _count += n
    return first


S_Q = _take(7)
S_KV = _take(16)
S_FWD = _take(4)
S_W = _take(1)
S_EW = _take(3)
S_WZ = _take(4)
S_W1 = _take(16)
S_W2 = _take(16)
S_W3 = _take(16)
S_WF = _take(16)
S_P = _take(8)
S_OUT = _take(2 * BLOCKS)
S_G1 = _take(NCH)
S_G2 = _take(NCH)
S_G3 = _take(NCH)
S_RELAY2 = _take(6)
S_PLUS2 = _take(6)
S_MINUS2 = _take(6)
S_EARLY = _take(BLOCKS)
S_RELAY3 = _take(2)
S_PLUS3 = _take(2)
S_MINUS3 = _take(2)
S_BACK = _take(2 * BLOCKS)
N_SEM = _count

L_Q = 0
L_KV = 3
L_W = 7
L_G = 8
L_U = 9
L_D = 10
L_RES = 11
L_ATT = 12
L_OUT = L_ATT + NCH
N_LOC = L_OUT + NCH


def layer(
    q_in, k_in, v_in, res_in, w_in, g_in, u_in, d_in, gain_ref, ids_ref, gates_ref, slots_ref,
    both_out,
    qb, kv, wb, wa_part, wb_part, gub, db, res, heads, proj, send_a, send_b, recv_a, recv_b, att, lay,
    place, comb_hi, comb_lo, gain_b,
    disp, xr, xall, acc, hid, ypart, relay2, plus2, minus2, yb, eb,
    early, stacks, relay3, plus3, minus3,
    ssem, rsem, lsem, ready,
):
    ctx = lax.axis_index("ctx")
    ex = lax.axis_index("exp")
    z, c = ctx // 2, ctx % 2
    x, y = ex // 4, ex % 4

    za, zb, zc = z + 1 - 2 * lax.rem(z, 2), NZ - 1 - z, lax.rem(z + 2, NZ)
    dev_a, dev_b = (za * 2 + c, ex), (zb * 2 + c, ex)

    def at_z(d):
        return (lax.rem(z + d + NZ, NZ) * 2 + c, ex)

    def at_x(d):
        return (ctx, lax.rem(x + d + 4, 4) * 4 + y)

    def at_y(d):
        return (ctx, x * 4 + lax.rem(y + d + 4, 4))

    def at_xy(n, sign=1):
        return (ctx, lax.rem(x + sign * (n // 4) + 4, 4) * 4 + lax.rem(y + sign * (n % 4) + 4, 4))

    plane = sorted(range(1, BLOCKS), key=lambda n: -min(n // 4, 4 - n // 4) - min(n % 4, 4 - n % 4))

    other = (z * 2 + 1 - c, ex)

    barrier = pltpu.get_barrier_semaphore()
    peers = [other] + [at(d) for at in (at_z, at_x, at_y) for d in (1, 2, 3)]
    for peer in peers:
        pl.semaphore_signal(barrier, inc=1, device_id=peer, device_id_type=MESH)

    def local(src, dst, n):
        return pltpu.make_async_copy(src, dst, lsem.at[n])

    sent = []

    def remote(src, dst, n, dev):
        return pltpu.make_async_remote_copy(
            src_ref=src, dst_ref=dst, send_sem=ssem.at[n], recv_sem=rsem.at[n],
            device_id=dev, device_id_type=MESH,
        )

    def send(src, dst, n, dev):
        copy = remote(src, dst, n, dev)
        copy.start()
        sent.append(copy)
        return copy

    mine = (2 * z + c) * TOK
    my_rows = pl.ds(pl.multiple_of(mine, TOK), TOK)

    def kv_parts():
        for h in range(2):
            for i, src in enumerate((k_in, v_in)):
                yield 2 * h + i, src.at[:, pl.ds(h * HD, HD)], kv.at[h, my_rows, pl.ds(i * HD, HD)]

    own_kv = [local(src, dst, L_KV + n) for n, src, dst in kv_parts()]

    def q_lanes(group):
        return q_in.at[:, pl.ds(pl.multiple_of(group * HW, HW), HW)]

    own_q = [local(q_lanes(g), qb.at[slot], L_Q + i) for i, (slot, g) in enumerate(((1, z), (4, za), (5, zb)))]
    w_rows = pl.ds(pl.multiple_of(c * K_DEV, K_DEV), K_DEV)
    own_w = local(w_in, wb.at[w_rows], L_W)
    g_rows = pl.ds(pl.multiple_of(c * FF_DEV, FF_DEV), FF_DEV)
    u_rows = pl.ds(pl.multiple_of(FF_CHIP + c * FF_DEV, FF_DEV), FF_DEV)
    own_g = local(g_in, gub.at[g_rows], L_G)
    own_u = local(u_in, gub.at[u_rows], L_U)
    own_d = local(d_in, db.at[g_rows], L_D)
    own_res = local(res_in, res, L_RES)
    for copy in (*own_kv, *own_q, own_w, own_res, own_g, own_u, own_d):
        copy.start()

    pl.semaphore_wait(barrier, len(peers))
    for d in (1, 2, 3):
        pl.semaphore_signal(ready, inc=1, device_id=at_x(d), device_id_type=MESH)

    row0 = c * K_DEV

    def w_part(buf, first, count, rnd, lane=0, lanes=CW):
        return buf.at[pl.ds(pl.multiple_of(row0 + first, 32), count), pl.ds(rnd * CW + lane, lanes)]

    ways = (
        (wa_part, 0, dev_a, 4 * x + y, x, at_y, at_x),
        (wb_part, D // 2, dev_b, 4 * y + x, y, at_x, at_y),
    )

    def w_step0(rnd):
        for i, (buf, lane, dev, piece, _, _, _) in enumerate(ways):
            first = pl.multiple_of(32 * piece, 32)
            src = w_in.at[pl.ds(first, 32), pl.ds(lane + rnd * CW, CW)]
            yield remote(src, w_part(buf, first, 32, rnd), S_WZ + 2 * rnd + i, dev)

    def w_step1(rnd):
        for i, (buf, _, _, piece, _, at1, _) in enumerate(ways):
            for d in (2, 1, 3):
                ref = w_part(buf, 32 * piece, 32, rnd)
                yield remote(ref, ref, S_W1 + 8 * rnd + 4 * i + d, at1(d))

    def w_step2(rnd):
        for i, (buf, _, _, _, block, _, at2) in enumerate(ways):
            for d in (1, 3):
                ref = w_part(buf, 128 * block, 128, rnd)
                yield remote(ref, ref, S_W2 + 8 * rnd + 4 * i + d, at2(d))

    def w_step3(rnd):
        for i, (buf, _, _, _, block, _, at2) in enumerate(ways):
            for d in (1, 3):
                ref = w_part(buf, 128 * lax.rem(block + 4 - d, 4), 128, rnd, (d // 2) * (CW // 2), CW // 2)
                yield remote(ref, ref, S_W3 + 8 * rnd + 4 * i + d, at2(d))

    def w_swap(rnd, which):
        for i, (buf, _, _, _, block, _, _) in enumerate(ways):
            for d in which:
                ref = w_part(buf, 128 * lax.rem(block + 4 - d, 4), 128, rnd)
                yield remote(ref, ref, S_WF + 8 * rnd + 4 * i + d, other)

    def begin(copies):
        for copy in copies:
            copy.start()

    def arrive(copies):
        for copy in copies:
            copy.wait_recv()

    begin(w_step0(0))
    kv_copies = {
        d: [send(src, dst, S_KV + 4 * d + n, at_z(d)) for n, src, dst in kv_parts()] for d in (2, 1, 3)
    }
    begin(w_step0(1))
    q_copies = [
        send(q_lanes(group), qb.at[slot], S_Q + slot, dev)
        for slot, group, dev in ((0, zb, dev_b), (2, za, dev_a), (3, zc, dev_b), (6, zc, dev_a))
    ]
    w_copy = send(w_in, wb.at[w_rows], S_W, other)

    for h in range(2):
        kv[h, :, pl.ds(2 * HD, HD)] = jnp.ones((SEQ, HD), BF16)
    ids = ids_ref[...]
    slots = slots_ref[...]
    gates = gates_ref[...]
    dest = ((ids // 4 - x) & 3) * 64 + (((ids & 3) - y) & 3) * 16 + slots
    dest = jnp.where(slots >= 0, dest, -16)
    row = lax.broadcasted_iota(jnp.int32, (STACK, TOK), 0)
    for quarter in range(4):
        placing = jnp.zeros((STACK, TOK), F32)
        combine = jnp.zeros((STACK, TOK), F32)
        for k in range(8):
            hit = row == dest[k : k + 1] + 4 * quarter
            placing += jnp.where(hit, 1.0, 0.0)
            combine += jnp.where(hit, gates[k : k + 1], 0.0)
        place[quarter] = placing.astype(BF16)
        combine = combine.T
        high = combine.astype(BF16)
        comb_hi[quarter] = high
        comb_lo[quarter] = (combine - high.astype(F32)).astype(BF16)
    gain_b[...] = jnp.broadcast_to(gain_ref[...], (8, D))

    for copy in own_kv:
        copy.wait()
    kv_lanes = pl.ds(0, 2 * HD)
    fwd = [send(kv.at[:, my_rows, kv_lanes], kv.at[:, my_rows, kv_lanes], S_FWD, other)]
    arrive(w_step0(0))
    begin(w_step1(0))
    for d in (1, 3, 2):
        arrive(kv_copies[d])
        rows = pl.ds(pl.multiple_of((lax.rem(z - d + NZ, NZ) * 2 + c) * TOK, TOK), TOK)
        fwd.append(send(kv.at[:, rows, kv_lanes], kv.at[:, rows, kv_lanes], S_FWD + d, other))
    arrive(w_step0(1))
    begin(w_step1(1))
    arrive(w_step1(0))
    begin(w_step2(0))
    begin(w_swap(0, (0,)))
    ew_copies = (
        send(g_in, gub.at[g_rows], S_EW, other),
        send(u_in, gub.at[u_rows], S_EW + 1, other),
        send(d_in, db.at[g_rows], S_EW + 2, other),
    )
    arrive(fwd)

    scale = HD**-0.5

    def attend(slot, owner, head):
        limit = c * TOK + lax.broadcasted_iota(jnp.int32, (TOK, 2 * TOK), 0)
        seen = lax.broadcasted_iota(jnp.int32, (TOK, 2 * TOK), 1) <= limit
        for v in range(NZ):

            @pl.when(owner == v)
            def _():
                keys = kv[head, pl.ds(0, 2 * TOK * (v + 1)), pl.ds(0, HD)]
                vals = kv[head, pl.ds(0, 2 * TOK * (v + 1)), pl.ds(HD, 2 * HD)]
                for h in range(HEADS):
                    lanes = pl.ds(h * HD, HD)
                    s = lax.dot_general(qb[slot, :, lanes], keys, NT, preferred_element_type=F32)
                    tail = jnp.where(seen, s[:, 2 * TOK * v :], -jnp.inf)
                    s = tail if v == 0 else jnp.concatenate([s[:, : 2 * TOK * v], tail], axis=1)
                    top = jnp.max(s, axis=1, keepdims=True)
                    p = jnp.exp((s - top) * scale).astype(BF16)
                    o = jnp.dot(p, vals, preferred_element_type=F32)
                    heads[pl.ds(pl.multiple_of(slot * TOK, TOK), TOK), lanes] = (o[:, :HD] / o[:, HD:]).astype(BF16)

    order = (1, 4, 5, 0, 2, 3, 6)
    owners = (zb, z, za, zb, z, z, za)
    groups = (z, z, z, za, za, zb, zb)

    def choose(step, values):
        out = values[order[0]]
        for n in range(1, 7):
            out = jnp.where(step == n, values[order[n]], out)
        return out

    for copy in own_q:
        copy.wait()

    def step_body(step, _):
        slot = choose(step, tuple(range(7)))

        @pl.when(step >= 3)
        def _():
            pltpu.make_async_copy(qb.at[1], qb.at[slot], rsem.at[S_Q + slot]).wait()

        attend(slot, choose(step, owners), choose(step, groups) // 2)

        @pl.when(step == 2)
        def _():
            arrive(w_step2(0))
            begin(w_step3(0))
            begin(w_swap(0, (1, 3)))
            arrive(w_step1(1))
            begin(w_step2(1))
            begin(w_swap(1, (0,)))

        return 0

    lax.fori_loop(0, 7, step_body, 0)

    def p_a(j, i):
        lanes = pl.ds(j * CW + i * QW, QW)
        return remote(send_a.at[:, lanes], recv_a.at[:, lanes], S_P + 2 * j + i, dev_b)

    def p_b(j, i):
        lanes = pl.ds((j - 2) * CW + i * QW, QW)
        return remote(send_b.at[:, lanes], recv_b.at[:, lanes], S_P + 2 * j + i, dev_a)

    def project(rnd):
        for i in range(2):
            lanes = pl.ds(rnd * CW + i * QW, QW)
            out = jnp.dot(heads[pl.ds(0, 2 * TOK), :], wb[:, lanes], preferred_element_type=F32)
            out += jnp.dot(heads[pl.ds(3 * TOK, 2 * TOK), :], wa_part[:, lanes], preferred_element_type=F32)
            send_a[:, lanes] = out[:TOK].astype(BF16)
            p_a(rnd, i).start()
            proj[:, lanes] = out[TOK:]
            wide = pl.ds(D // 2 + rnd * CW + i * QW, QW)
            out = jnp.dot(heads[pl.ds(TOK, 2 * TOK), :], wb[:, wide], preferred_element_type=F32)
            out += jnp.dot(heads[pl.ds(5 * TOK, 2 * TOK), :], wb_part[:, lanes], preferred_element_type=F32)
            send_b[:, lanes] = out[TOK:].astype(BF16)
            p_b(2 + rnd, i).start()
            proj[:, wide] = out[:TOK]
            sent.extend([p_a(rnd, i), p_b(2 + rnd, i)])

    def pick(quarter, stacked_axis):
        shape = (ROWS, STACK) if stacked_axis else (STACK, ROWS)
        at = lax.broadcasted_iota(jnp.int32, shape, stacked_axis)
        slot_row = lax.broadcasted_iota(jnp.int32, shape, 1 - stacked_axis)
        return jnp.where(at == (slot_row // 4) * 16 + 4 * quarter + slot_row % 4, 1.0, 0.0).astype(BF16)

    own_res.wait()
    pl.semaphore_wait(ready, 3)
    square = jnp.zeros((TOK, 1), F32)
    own_copies = []

    def out_copy(p, n):
        rows = pl.ds(16 * n, 16)
        return remote(disp.at[rows, qcols(p)], xr.at[rows, qcols(p)], S_OUT + BLOCKS * p + n, at_xy(n))

    def g1(j):
        return remote(xall.at[pl.ds(0, ROWS), xcols(j)], xall.at[pl.ds(ROWS, ROWS), xcols(j)], S_G1 + j, at_z(1))

    def g3(j):
        return remote(xall.at[pl.ds(0, ROWS), xcols(j)], xall.at[pl.ds(3 * ROWS, ROWS), xcols(j)], S_G3 + j, at_z(-1))

    def g2(j):
        slot, way = (1, 1) if j < 2 else (3, -1)
        return remote(
            xall.at[pl.ds(slot * ROWS, ROWS), xcols(j)], xall.at[pl.ds(2 * ROWS, ROWS), xcols(j)], S_G2 + j, at_z(way)
        )

    def start(copies):
        for copy in copies:
            copy.start()
            sent.append(copy)

    def attended_chunk(j, square):
        for i in range(2):
            (p_a if j < 2 else p_b)(j, i).wait_recv()
        lanes = pl.ds((j % 2) * CW, CW)
        total = proj[:, cols(j)] + (recv_a if j < 2 else recv_b)[:, lanes].astype(F32)
        a = (res[:, cols(j)].astype(F32) + total).astype(BF16)
        att[:, cols(j)] = a
        copy = local(att.at[:, cols(j)], both_out.at[0, :, cols(j)], L_ATT + j)
        copy.start()
        own_copies.append(copy)
        a = a.astype(F32)
        square += jnp.sum(a * a, axis=1, keepdims=True)
        scaled = (a * gain_b[pl.ds(0, 1), cols(j)]).astype(BF16)
        return square, scaled

    def dispatch_half(p, square):
        stack = jnp.zeros((STACK, QW), F32)
        for j in (p, 2 + p):
            square, scaled = attended_chunk(j, square)
            for i in range(2):
                stack += jnp.dot(place[2 * (j // 2) + i], scaled[:, i * QW : (i + 1) * QW], preferred_element_type=F32)
        stack = stack.astype(BF16)
        disp[:, pl.ds(p * QW, QW)] = stack
        xr[pl.ds(0, 16), pl.ds(p * QW, QW)] = stack[:16]
        if p == 1:
            norm = lax.rsqrt(square * (1.0 / D) + 1e-06)
            norm = jnp.broadcast_to(norm, (TOK, SCALE_COLS))
            norm_hi = norm.astype(BF16).astype(F32)
            lane = lax.broadcasted_iota(jnp.int32, (TOK, SCALE_COLS), 1)
            both = jnp.where(lane < SCALE_COLS // 2, norm_hi, norm - norm_hi).astype(BF16)
            stack = jnp.dot(place[0], both, preferred_element_type=F32).astype(BF16)
            disp[:, pl.ds(2 * QW, SCALE_COLS)] = stack
            xr[pl.ds(0, 16), pl.ds(2 * QW, SCALE_COLS)] = stack[:16]
        start([out_copy(p, n) for n in plane])
        return square

    def gather_half(p):
        for n in plane:
            out_copy(p, n).wait_recv()
        stack = xr[:, pl.ds(p * QW, QW)]
        for quarter in range(4):
            rows = jnp.dot(pick(quarter, 1), stack, preferred_element_type=F32).astype(BF16)
            xall[pl.ds(0, ROWS), pl.ds((quarter // 2) * HALF + p * CW + (quarter % 2) * QW, QW)] = rows
        if p == 1:
            rows = jnp.dot(pick(0, 1), xr[:, pl.ds(2 * QW, SCALE_COLS)], preferred_element_type=F32).astype(BF16)
            xall[pl.ds(0, ROWS), pl.ds(D, SCALE_COLS)] = rows
        for j in (p, 2 + p):
            start([g1(j), g3(j)])

    def pass_chunk(j):
        (g1(j) if j < 2 else g3(j)).wait_recv()
        start([g2(j)])

    def gate_up_chunk(j):
        (g3(j) if j < 2 else g1(j)).wait_recv()
        g2(j).wait_recv()
        prod = lax.dot_general(xall[:, cols(j)], gub[:, cols(j)], NT, preferred_element_type=F32)
        acc[...] = prod if j == 0 else acc[...] + prod

    own_w.wait()
    w_copy.wait_recv()
    arrive(w_step3(0))
    begin(w_swap(0, (2,)))
    arrive(w_swap(0, (0, 1, 3, 2)))
    project(0)
    arrive(w_step2(1))
    begin(w_step3(1))
    begin(w_swap(1, (1, 3)))
    square = dispatch_half(0, square)
    arrive(w_step3(1))
    begin(w_swap(1, (2,)))
    arrive(w_swap(1, (0, 1, 3, 2)))
    project(1)
    for rnd in (0, 1):
        for copies in (w_step0(rnd), w_step1(rnd), w_step2(rnd), w_step3(rnd), w_swap(rnd, (0, 1, 2, 3))):
            sent.extend(copies)
    gather_half(0)
    square = dispatch_half(1, square)
    for j in (0, 2):
        pass_chunk(j)
    gather_half(1)
    own_g.wait()
    own_u.wait()
    own_d.wait()
    for copy in ew_copies:
        copy.wait_recv()
    for j in (0, 2):
        gate_up_chunk(j)
    for j in (1, 3):
        pass_chunk(j)
    for j in (1, 3):
        gate_up_chunk(j)

    sc = xall[:, pl.ds(D, SCALE_COLS)].astype(F32)
    sc = sc[:, 0:1] + sc[:, SCALE_COLS // 2 : SCALE_COLS // 2 + 1]
    gate = acc[:, pl.ds(0, FF_CHIP)] * sc
    upper = acc[:, pl.ds(FF_CHIP, FF_CHIP)] * sc
    hid[...] = (gate * jax.nn.sigmoid(gate) * upper).astype(BF16)

    def unit(u):
        return pl.ds(u * QW, QW)

    def q_relay2(u):
        return remote(
            ypart.at[pl.ds(2 * ROWS, ROWS), unit(u)], relay2.at[:, unit(u)], S_RELAY2 + u, at_z(1 if u % 2 == 0 else -1)
        )

    def q_plus2(u):
        return remote(ypart.at[pl.ds(ROWS, ROWS), unit(u)], plus2.at[:, unit(u)], S_PLUS2 + u, at_z(-1))

    def q_minus2(u):
        return remote(ypart.at[pl.ds(3 * ROWS, ROWS), unit(u)], minus2.at[:, unit(u)], S_MINUS2 + u, at_z(1))

    def early_copy(n):
        rows = pl.ds(16 * n, 16)
        return remote(early.at[rows], stacks.at[rows], S_EARLY + n, at_xy(n, -1))

    def third(half):
        return pl.ds(half * (EW // 2), EW // 2)

    def slot_lanes(slot, half):
        return pl.ds(slot * EW + half * (EW // 2), EW // 2)

    def r_relay(half):
        return remote(
            stacks.at[:, slot_lanes(2, half)], relay3.at[:, third(half)], S_RELAY3 + half, at_z(1 if half == 0 else -1)
        )

    def r_plus(half):
        return remote(stacks.at[:, slot_lanes(1, half)], plus3.at[:, third(half)], S_PLUS3 + half, at_z(-1))

    def r_minus(half):
        return remote(stacks.at[:, slot_lanes(3, half)], minus3.at[:, third(half)], S_MINUS3 + half, at_z(1))

    for j in range(NCH - 1):
        ypart[:, cols(j)] = jnp.dot(hid[...], db[:, cols(j)], preferred_element_type=F32).astype(BF16)
        start([q_relay2(2 * j), q_relay2(2 * j + 1)])
    start([q_plus2(0), q_minus2(1)])
    last = jnp.dot(hid[...], db[:, cols(NCH - 1)], preferred_element_type=F32).astype(BF16)
    for slot in range(NZ):
        stack = jnp.zeros((STACK, EW), F32)
        for quarter in range(4):
            rows = last[slot * ROWS : (slot + 1) * ROWS, quarter * EW : (quarter + 1) * EW]
            stack += jnp.dot(pick(quarter, 0), rows, preferred_element_type=F32)
        stack = stack.astype(BF16)
        early[:, pl.ds(slot * EW, EW)] = stack
        stacks[pl.ds(0, 16), pl.ds(slot * EW, EW)] = stack[:16]
    start([early_copy(n) for n in plane])
    for u in range(6):
        joined, copy, direct = (3, q_minus2, q_plus2) if u % 2 == 0 else (1, q_plus2, q_minus2)
        q_relay2(u).wait_recv()
        rows = pl.ds(joined * ROWS, ROWS)
        ypart[rows, unit(u)] = (ypart[rows, unit(u)].astype(F32) + relay2[:, unit(u)].astype(F32)).astype(BF16)
        start([copy(u)])
        if u >= 2:
            start([direct(u)])

    widths = (QW, EW)

    def back_copy(p, n):
        rows = pl.ds(16 * n, 16)
        lanes = pl.ds(p * QW, widths[p])
        return remote(yb.at[rows, lanes], eb.at[rows, lanes], S_BACK + BLOCKS * p + n, at_xy(n, -1))

    def return_part(p):
        width = widths[p]
        stack = jnp.zeros((STACK, width), F32)
        quarter = 0
        for u in ((0, 1, 2, 3), (4, 5))[p]:
            q_plus2(u).wait_recv()
            q_minus2(u).wait_recv()
            rows = (
                ypart[pl.ds(0, ROWS), unit(u)].astype(F32)
                + plus2[:, unit(u)].astype(F32)
                + minus2[:, unit(u)].astype(F32)
            ).astype(BF16)
            for i in range(QW // width):
                part = rows[:, i * width : (i + 1) * width]
                stack += jnp.dot(pick(quarter, 0), part, preferred_element_type=F32)
                quarter += 1
        stack = stack.astype(BF16)
        lanes = pl.ds(p * QW, width)
        yb[:, lanes] = stack
        eb[pl.ds(0, 16), lanes] = stack[:16]
        start([back_copy(p, n) for n in plane])

    def combine_stack(p, first, width, stack):
        for quarter in range(4):
            lanes = pl.ds(first + quarter * width, width)
            moe = jnp.dot(comb_hi[quarter], stack, preferred_element_type=F32)
            moe += jnp.dot(comb_lo[quarter], stack, preferred_element_type=F32)
            lay[:, lanes] = (att[:, lanes].astype(F32) + moe).astype(BF16)
        lanes = pl.ds(first, 4 * width)
        copy = local(lay.at[:, lanes], both_out.at[1, :, lanes], L_OUT + p)
        copy.start()
        own_copies.append(copy)

    def combine_part(p):
        for n in plane:
            back_copy(p, n).wait_recv()
        combine_stack(p, p * HALF, widths[p], eb[:, pl.ds(p * QW, widths[p])])

    return_part(0)
    for n in plane:
        early_copy(n).wait_recv()
    start([r_relay(0), r_relay(1), r_plus(0), r_minus(1)])
    return_part(1)
    for half, slot, copy in ((0, 3, r_minus), (1, 1, r_plus)):
        r_relay(half).wait_recv()
        lanes = slot_lanes(slot, half)
        stacks[:, lanes] = (stacks[:, lanes].astype(F32) + relay3[:, third(half)].astype(F32)).astype(BF16)
        start([copy(half)])
    combine_part(0)
    combine_part(1)
    for half in (0, 1):
        r_plus(half).wait_recv()
        r_minus(half).wait_recv()
    stack = (
        stacks[:, pl.ds(0, EW)].astype(F32) + plus3[...].astype(F32) + minus3[...].astype(F32)
    ).astype(BF16)
    combine_stack(2, 3 * CW, EW, stack)

    for copy in own_copies:
        copy.wait()
    for copy in sent:
        copy.wait_send()


def shards(
    queries, keys, values, residual, out_weight, norm_gain, expert_ids, gate_weights, slots, w_gate, w_up, w_down
):
    out = jax.ShapeDtypeStruct((2, TOK, D), BF16)
    hbm = pl.BlockSpec(memory_space=pl.ANY)
    vmem = pl.BlockSpec(memory_space=pltpu.VMEM)

    def buf(*shape, dtype=BF16):
        return pltpu.VMEM(shape, dtype)

    both = pl.pallas_call(
        layer,
        out_shape=out,
        in_specs=[hbm] * 8 + [vmem] * 4,
        out_specs=hbm,
        scratch_shapes=[
            buf(7, TOK, HW),
            buf(2, SEQ, 3 * HD),
            buf(2 * K_DEV, D),
            buf(2 * K_DEV, D // 2),
            buf(2 * K_DEV, D // 2),
            buf(2 * FF_CHIP, D),
            buf(FF_CHIP, D),
            buf(TOK, D),
            buf(7 * TOK, HW),
            buf(TOK, D, dtype=F32),
            buf(TOK, D // 2),
            buf(TOK, D // 2),
            buf(TOK, D // 2),
            buf(TOK, D // 2),
            buf(TOK, D),
            buf(TOK, D),
            buf(4, STACK, TOK),
            buf(4, TOK, STACK),
            buf(4, TOK, STACK),
            buf(8, D, dtype=F32),
            buf(STACK, 2 * QW + SCALE_COLS),
            buf(STACK, 2 * QW + SCALE_COLS),
            buf(NZ * ROWS, DX),
            buf(NZ * ROWS, 2 * FF_CHIP, dtype=F32),
            buf(NZ * ROWS, FF_CHIP),
            buf(NZ * ROWS, D),
            buf(ROWS, D),
            buf(ROWS, D),
            buf(ROWS, D),
            buf(STACK, 2 * QW),
            buf(STACK, 2 * QW),
            buf(STACK, 4 * EW),
            buf(STACK, 4 * EW),
            buf(STACK, EW),
            buf(STACK, EW),
            buf(STACK, EW),
            pltpu.SemaphoreType.DMA((N_SEM,)),
            pltpu.SemaphoreType.DMA((N_SEM,)),
            pltpu.SemaphoreType.DMA((N_LOC,)),
            pltpu.SemaphoreType.REGULAR,
        ],
        compiler_params=pltpu.CompilerParams(collective_id=0, has_side_effects=True, vmem_limit_bytes=56 << 20),
        name="decoder_layer",
    )(
        queries[0], keys[0], values[0], residual[0], out_weight,
        w_gate[0].T, w_up[0].T, w_down[0], norm_gain[None],
        expert_ids[0].T, gate_weights[0].T, slots[0].T,
    )
    return both[:1], both[1:]


def solution(mesh):
    rows = P("exp", "ctx", None)
    placed = (rows, rows, rows, rows, P("ctx", None), P(), rows, rows, rows,
              P("exp", None, "ctx"), P("exp", None, "ctx"), rows)
    return jax.shard_map(shards, mesh=mesh, in_specs=placed, out_specs=(rows, rows), check_vma=False)
```

profile of v0, /device:TPU:0, one launch (start us, length us, event | category | flops | bytes accessed | tf_op | source)
XLA Modules:
  0.0 106.0 jit_solution(8957294020713881465)
XLA Ops:
  0.6 102.3 %decoder_layer.1 = bf16[2,128,4096]{2,1,0:T(8,128)(2,1)} custom-call(bf16[128,4096]{1,0:T(8,128)(2,1)} %bitcast.24, bf16[128,256]{1,0:T(8,128)(2,1)} %bitcast.26, bf16[128,256]{1,0:T(8,128)(2,1)} %bitcast.27, bf16[128,4096]{1,0:T(8,128)(2,1)} %bitcast.25, bf16[512,4096]{1,0:T(8,128)(2,1)} %w_in.1, bf16[192,4096]{1,0:T(8,128)(2,1)} %bitcast.21, ...), custom_call_target="tpu_custom_call" | custom-call | tf_op jit(solution)/shard_map/decoder_layer/pallas_call | solution.py:635
  102.9 3.1 %fusion = (bf16[1,128,4096]{2,1,0:T(8,128)(2,1)}, bf16[1,128,4096]{2,1,0:T(8,128)(2,1)}) fusion(bf16[2,128,4096]{2,1,0:T(8,128)(2,1)} %decoder_layer.1), kind=kLoop, calls=%fused_computation | loop fusion | bytes 4194304 | tf_op jit(solution)/shard_map/slice | solution.py:689
where the time goes:
time: 106 us
  Pallas kernels  102 us (96%)
  local copies, waits for them, and re-layouts  3.08 us (3%)
    pallas_call x1, Pallas kernels, shards(): pl.pallas_call(layer, out_shape=out, in_specs=[hbm] * 8 + [vmem] * 4, out...  102 us
    slice x1, local copies, waits for them, and re-layouts, shards(): return (both[:1], both[1:])  3.08 us

commit v1 on v0

--- a/solution.py
+++ b/solution.py
@@ -228,10 +228,10 @@
             copy.wait_recv()
 
     begin(w_step0(0))
+    begin(w_step0(1))
     kv_copies = {
         d: [send(src, dst, S_KV + 4 * d + n, at_z(d)) for n, src, dst in kv_parts()] for d in (2, 1, 3)
     }
-    begin(w_step0(1))
     q_copies = [
         send(q_lanes(group), qb.at[slot], S_Q + slot, dev)
         for slot, group, dev in ((0, zb, dev_b), (2, za, dev_a), (3, zc, dev_b), (6, zc, dev_a))
@@ -266,12 +266,12 @@
     fwd = [send(kv.at[:, my_rows, kv_lanes], kv.at[:, my_rows, kv_lanes], S_FWD, other)]
     arrive(w_step0(0))
     begin(w_step1(0))
+    arrive(w_step0(1))
+    begin(w_step1(1))
     for d in (1, 3, 2):
         arrive(kv_copies[d])
         rows = pl.ds(pl.multiple_of((lax.rem(z - d + NZ, NZ) * 2 + c) * TOK, TOK), TOK)
         fwd.append(send(kv.at[:, rows, kv_lanes], kv.at[:, rows, kv_lanes], S_FWD + d, other))
-    arrive(w_step0(1))
-    begin(w_step1(1))
     arrive(w_step1(0))
     begin(w_step2(0))
     begin(w_swap(0, (0,)))

time: 106 us -> 104 us (0.981)
  Pallas kernels: 102 us -> 100 us
    pallas_call x1, Pallas kernels: 102 us -> 100 us  [shards(): pl.pallas_call(layer, out_shape=out, in_specs=[hbm] * 8 + [vmem] * 4, out...]
where the time goes in v1:
time: 104 us
  Pallas kernels  100 us (96%)
  local copies, waits for them, and re-layouts  3.08 us (3%)
    pallas_call x1, Pallas kernels, shards(): pl.pallas_call(layer, out_shape=out, in_specs=[hbm] * 8 + [vmem] * 4, out...  100 us
    slice x1, local copies, waits for them, and re-layouts, shards(): return (both[:1], both[1:])  3.08 us

profile of v1, /device:TPU:0, one launch (start us, length us, event | category | flops | bytes accessed | tf_op | source)
XLA Modules:
  0.0 104.1 jit_solution(3972763518443061127)
XLA Ops:
  0.6 100.4 %decoder_layer.1 = bf16[2,128,4096]{2,1,0:T(8,128)(2,1)} custom-call(bf16[128,4096]{1,0:T(8,128)(2,1)} %bitcast.24, bf16[128,256]{1,0:T(8,128)(2,1)} %bitcast.26, bf16[128,256]{1,0:T(8,128)(2,1)} %bitcast.27, bf16[128,4096]{1,0:T(8,128)(2,1)} %bitcast.25, bf16[512,4096]{1,0:T(8,128)(2,1)} %w_in.1, bf16[192,4096]{1,0:T(8,128)(2,1)} %bitcast.21, ...), custom_call_target="tpu_custom_call" | custom-call | tf_op jit(solution)/shard_map/decoder_layer/pallas_call | solution.py:635
  101.0 3.1 %fusion = (bf16[1,128,4096]{2,1,0:T(8,128)(2,1)}, bf16[1,128,4096]{2,1,0:T(8,128)(2,1)}) fusion(bf16[2,128,4096]{2,1,0:T(8,128)(2,1)} %decoder_layer.1), kind=kLoop, calls=%fused_computation | loop fusion | bytes 4194304 | tf_op jit(solution)/shard_map/slice | solution.py:689

commit v2 on v1

--- a/solution.py
+++ b/solution.py
@@ -275,11 +275,6 @@
     arrive(w_step1(0))
     begin(w_step2(0))
     begin(w_swap(0, (0,)))
-    ew_copies = (
-        send(g_in, gub.at[g_rows], S_EW, other),
-        send(u_in, gub.at[u_rows], S_EW + 1, other),
-        send(d_in, db.at[g_rows], S_EW + 2, other),
-    )
     arrive(fwd)
 
     scale = HD**-0.5
@@ -467,6 +462,11 @@
     begin(w_swap(1, (2,)))
     arrive(w_swap(1, (0, 1, 3, 2)))
     project(1)
+    ew_copies = (
+        send(g_in, gub.at[g_rows], S_EW, other),
+        send(u_in, gub.at[u_rows], S_EW + 1, other),
+        send(d_in, db.at[g_rows], S_EW + 2, other),
+    )
     for rnd in (0, 1):
         for copies in (w_step0(rnd), w_step1(rnd), w_step2(rnd), w_step3(rnd), w_swap(rnd, (0, 1, 2, 3))):
             sent.extend(copies)

time: 104 us -> 104 us (level)
  no operation moved by 1% of the time
where the time goes in v2:
time: 104 us; the launch traced here: 103 us
  Pallas kernels  99.7 us (96%)
  local copies, waits for them, and re-layouts  3.08 us (3%)
    pallas_call x1, Pallas kernels, shards(): pl.pallas_call(layer, out_shape=out, in_specs=[hbm] * 8 + [vmem] * 4, out...  99.7 us
    slice x1, local copies, waits for them, and re-layouts, shards(): return (both[:1], both[1:])  3.08 us

profile of v2, /device:TPU:0, one launch (start us, length us, event | category | flops | bytes accessed | tf_op | source)
XLA Modules:
  0.0 103.4 jit_solution(11390268330121691329)
XLA Ops:
  0.6 99.7 %decoder_layer.1 = bf16[2,128,4096]{2,1,0:T(8,128)(2,1)} custom-call(bf16[128,4096]{1,0:T(8,128)(2,1)} %bitcast.24, bf16[128,256]{1,0:T(8,128)(2,1)} %bitcast.26, bf16[128,256]{1,0:T(8,128)(2,1)} %bitcast.27, bf16[128,4096]{1,0:T(8,128)(2,1)} %bitcast.25, bf16[512,4096]{1,0:T(8,128)(2,1)} %w_in.1, bf16[192,4096]{1,0:T(8,128)(2,1)} %bitcast.21, ...), custom_call_target="tpu_custom_call" | custom-call | tf_op jit(solution)/shard_map/decoder_layer/pallas_call | solution.py:635
  100.3 3.1 %fusion = (bf16[1,128,4096]{2,1,0:T(8,128)(2,1)}, bf16[1,128,4096]{2,1,0:T(8,128)(2,1)}) fusion(bf16[2,128,4096]{2,1,0:T(8,128)(2,1)} %decoder_layer.1), kind=kLoop, calls=%fused_computation | loop fusion | bytes 4194304 | tf_op jit(solution)/shard_map/slice | solution.py:689
